TPU v7x, 256 devices: a whole 4x4x8 slice. The times are simulated.
256 devices in a mesh: work: 32 (over z, y_hi, core), tp: 8 (over x, y_lo).
Axes of the slice: x: 4, y: 4 (y_hi: 2, y_lo: 2; y = y_hi * 2 + y_lo), z: 8, core: 2. Of those that a mesh axis runs over, the one named last changes fastest.
Arguments:
- queries: bfloat16 [32, 16, 40, 128], P('work', None, 'tp'), may hold values from -6 to 6
- new_keys: bfloat16 [32, 16, 8, 128], P('work', None, 'tp'), may hold values from -24 to 24
- new_values: bfloat16 [32, 16, 8, 128], P('work', None, 'tp'), may hold values from -24 to 24
- cache_keys: bfloat16 [32, 4096, 8, 128], P('work', None, 'tp'), may hold values from -96 to 96
- cache_values: bfloat16 [32, 4096, 8, 128], P('work', None, 'tp'), may hold values from -24 to 24
- lengths: int32 [32], P('work'), may hold values from 1024 to 4096, as said below
- positions: int32 [32, 16], P('work'), may hold values from 0 to 32767, as said below
- out_weight: bfloat16 [5120, 5120], P('tp'), may hold values from -0.078125 to 0.078125
Outputs:
- layer_out: bfloat16 [32, 16, 5120], P('work', None, 'tp')
Inputs may be any that keep to these rules, and one draw needn't show every extreme that they name: `lengths`: every worker's cache holds at least 1024 live rows; some worker's cache is full and some holds exactly 1024. Each worker's new tokens have consecutive positions.
All inputs are finite; a program needn't handle non-finite values.
Results may differ from a plain program's by a relative error of at most 0.022.
The roundings to bfloat16 on the way count: a program that leaves them out, or rounds other values in their place, can miss the bound.
Values may be sent and summed in bfloat16 or wider, within the bound.
A program may use at most 192 MiB of HBM per device.

v0:
```python
import math

import jax
import jax.numpy as jnp
from jax import lax
from jax.experimental import pallas as pl
from jax.experimental.pallas import tpu as pltpu
from jax.sharding import PartitionSpec as P

MESH = pl.DeviceIdType.MESH
F32 = jnp.float32
BF16 = jnp.bfloat16

HEADS = 5
ROWS = 16
HD = 128
CACHE = 4096
PAIR = 2 * CACHE
NEWPAD = 128
BLOCK = HEADS * ROWS
GROUP = 2
PARTS = 2 * GROUP
TILE = PARTS * BLOCK
CHUNK = 2048
CHUNKS = PAIR // CHUNK
TP = 8
COLS = 640
PLANES = 8
TILES = PLANES // GROUP
ORDER = (0, 7, 3, 5, 4, 2, 6, 1)
CODE = sum(d * PLANES**i for i, d in enumerate(ORDER))
SLOTS = 2 * PLANES
MESSAGE = BLOCK + 16
LEAST = 1024
STEP = 1024

SCALE2 = HD**-0.5 * math.log2(math.e)
LOG_BASE = math.log(1000000.0)
NT = (((1,), (1,)), ((), ()))


def cos_sin(angle):
    turn = jnp.floor(angle * (2.0 / math.pi) + 0.5)
    rest = angle - turn * 1.5703125
    rest = rest - turn * 4.837512969970703125e-4
    rest = rest - turn * 7.54978995489188e-8
    z = rest * rest
    sine = rest + rest * z * ((-1.9515295891e-4 * z + 8.3321608736e-3) * z - 1.6666654611e-1)
    cosine = 1.0 - 0.5 * z + z * z * (
        (2.443315711809948e-5 * z - 1.388731625493765e-3) * z + 4.166664568298827e-2
    )
    quarter = turn.astype(jnp.int32) & 3
    odd = (quarter & 1) == 1
    c = jnp.where(odd, sine, cosine)
    s = jnp.where(odd, cosine, sine)
    c = jnp.where((quarter == 1) | (quarter == 2), -c, c)
    s = jnp.where(quarter >= 2, -s, s)
    return c, s


def kernel(
    pos_ref, len_ref, q_ref, nk_ref, nv_ref, ck_ref, cv_ref, w_ref, out_ref,
    kall, vaug, wv, qbuf, nsend, nrecv, s0, s1, t0, t1, mx0, mx1, acc,
    flat, psend, precv, lens,
    loc_sem, pair_send, pair_recv, q_send, q_recv, n_send, n_recv,
    p_send, p_recv,
):
    me = lax.axis_index("work")
    t = lax.axis_index("tp")
    z = me // 4
    yh = (me // 2) % 2
    c = me % 2

    def device(d, rel, core):
        hi = (yh + rel) % 2
        return {"work": 4 * ((z + d + PLANES) % PLANES) + 2 * hi + core, "tp": t}

    def remote(src, dst, send, recv, to):
        return pltpu.make_async_remote_copy(
            src, dst, send, recv, device_id=to, device_id_type=MESH
        )

    sibling = device(0, 0, 1 - c)
    partner = device(0, 1, c)

    copy_k = pltpu.make_async_copy(ck_ref, kall.at[pl.ds(0, CACHE)], loc_sem.at[0])
    copy_v = pltpu.make_async_copy(
        cv_ref, vaug.at[pl.ds(0, CACHE), pl.ds(0, HD)], loc_sem.at[1]
    )
    copy_k.start()
    copy_v.start()

    barrier = pltpu.get_barrier_semaphore()

    def signal(to):
        pl.semaphore_signal(barrier, inc=1, device_id=to, device_id_type=MESH)

    def greet(i, _):
        signal(device(i // 2, i % 2, c))
        return 0

    lax.fori_loop(1, SLOTS, greet, 0)
    signal(sibling)

    def greet_tp(i, _):
        signal({"work": me, "tp": (t + i) % TP})
        return 0

    lax.fori_loop(1, TP, greet_tp, 0)

    lane = lax.broadcasted_iota(jnp.int32, (ROWS, HD), 1)
    place = pos_ref[0] + lax.broadcasted_iota(jnp.int32, (ROWS, HD), 0)
    ladder = (lane % (HD // 2)).astype(F32) * (2.0 / HD)
    angle = place.astype(F32) * jnp.exp(ladder * -LOG_BASE)
    cosine, sine = cos_sin(angle)
    sine = jnp.where(lane < HD // 2, -sine, sine)

    def rotated(x):
        x = x.astype(F32)
        return (x * cosine + pltpu.roll(x, HD // 2, 1) * sine).astype(BF16)

    for g in range(HEADS):
        qbuf[0, g * ROWS : (g + 1) * ROWS, :] = rotated(q_ref[g * ROWS : (g + 1) * ROWS, :])
    kall[PAIR : PAIR + ROWS, :] = rotated(nk_ref[...])
    lens[0] = jnp.full((8, HD), len_ref[0], jnp.int32).astype(F32)

    pl.semaphore_wait(barrier, SLOTS - 1 + 1 + TP - 1)

    def query_copy(k, d, rel):
        return remote(qbuf.at[0], qbuf.at[k], q_send.at[k], q_recv.at[k], device(-d, rel, c))

    pair = [
        remote(src, dst, pair_send.at[k], pair_recv.at[k], sibling)
        for k, (src, dst) in enumerate(
            (
                (lens.at[0], lens.at[1]),
                (kall.at[pl.ds(PAIR, ROWS)], kall.at[pl.ds(PAIR + ROWS, ROWS)]),
                (nv_ref, vaug.at[pl.ds(PAIR + ROWS, ROWS), pl.ds(0, HD)]),
                (ck_ref, kall.at[pl.ds(CACHE, CACHE)]),
                (cv_ref, vaug.at[pl.ds(CACHE, CACHE), pl.ds(0, HD)]),
            )
        )
    ]
    query_copy(1, 0, 1).start()
    for copy in pair[:4]:
        copy.start()

    def send_queries(i, code):
        for rel in range(2):
            query_copy(2 * i + rel, code % PLANES, rel).start()
        return code // PLANES

    lax.fori_loop(1, PLANES, send_queries, CODE // PLANES)
    pair[4].start()

    def weight_copy(k):
        return pltpu.make_async_copy(
            w_ref.at[:, pl.ds(pl.multiple_of(k * COLS, HD), COLS)], wv.at[k], loc_sem.at[2 + k]
        )

    def start_weights(k, _):
        weight_copy(k).start()
        return 0

    lax.fori_loop(0, TP, start_weights, 0)

    kall[PAIR + 2 * ROWS :, :] = jnp.zeros((NEWPAD - 2 * ROWS, HD), BF16)
    vaug[PAIR : PAIR + ROWS, 0:HD] = nv_ref[...]
    vaug[PAIR + 2 * ROWS :, 0:HD] = jnp.zeros((NEWPAD - 2 * ROWS, HD), BF16)
    vaug[PAIR:, HD:] = jnp.ones((NEWPAD, HD), BF16)

    def live_rows(base, j):
        rows = lax.broadcasted_iota(jnp.int32, (STEP, HD), 0) + j * STEP
        return jnp.where(rows.astype(F32) < lens[base // CACHE, 0:1, :], 1.0, 0.0).astype(BF16)

    def mask_keys(base):
        first = kall[base : base + 16, :].astype(F32)[0:1, :]
        first = jnp.broadcast_to(first, (STEP, HD)).astype(BF16)

        def body(j, _):
            live = live_rows(base, j)
            rows = pl.ds(base + pl.multiple_of(j * STEP, STEP), STEP)
            kall[rows, :] = kall[rows, :] * live + first * (1.0 - live)
            return 0

        lax.fori_loop(LEAST // STEP, CACHE // STEP, body, 0)

    def mask_values(base):
        def ones(j, _):
            rows = pl.ds(base + pl.multiple_of(j * STEP, STEP), STEP)
            vaug[rows, HD:] = jnp.ones((STEP, HD), BF16)
            return 0

        lax.fori_loop(0, LEAST // STEP, ones, 0)

        def body(j, _):
            live = live_rows(base, j)
            rows = pl.ds(base + pl.multiple_of(j * STEP, STEP), STEP)
            vaug[rows, 0:HD] = vaug[rows, 0:HD] * live
            vaug[rows, HD:] = live
            return 0

        lax.fori_loop(LEAST // STEP, CACHE // STEP, body, 0)

    def wait_queries(i):
        for part in range(PARTS):
            query_copy(PARTS * i + part, 0, 1).wait_recv()

    def queries_of(i):
        return qbuf[pl.ds(PARTS * i, PARTS)].reshape(TILE, HD)

    def chunk(j):
        return pl.ds(pl.multiple_of(j * CHUNK, CHUNK), CHUNK)

    def scores(q, j, s_ref, mx):
        s = lax.dot_general(q, kall[chunk(j), :], NT, preferred_element_type=F32)
        s_ref[j] = s
        top = mx[...]
        for u in range(CHUNK // HD):
            top = jnp.maximum(top, s[:, u * HD : (u + 1) * HD])
        mx[...] = top

    def new_scores(first, q, t_ref, mx):
        row = lax.broadcasted_iota(jnp.int32, (TILE, HD), 0)
        col = lax.broadcasted_iota(jnp.int32, (TILE, HD), 1)
        r, r2 = row & 15, col & 15
        seen = (r2 >> 2) < (r >> 2)
        if first:
            own = (row < BLOCK) & (col < ROWS)
            seen = seen | (own & ((r2 >> 2) == (r >> 2)) & (r2 <= r))
        s = lax.dot_general(q, kall[PAIR:, :], NT, preferred_element_type=F32)
        s = jnp.where(seen & (col < 2 * ROWS), s, -1e30)
        t_ref[...] = s
        mx[...] = s

    def close_max(mx):
        mx[...] = jnp.broadcast_to(jnp.max(mx[...], axis=1, keepdims=True), (TILE, HD))

    def weights(s, top):
        return jnp.exp2((s - top) * SCALE2).astype(BF16)

    def chunk_weights(j, s_ref, mx):
        top = mx[...]
        return jnp.concatenate(
            [weights(s_ref[j, :, u * HD : (u + 1) * HD], top) for u in range(CHUNK // HD)], axis=1
        )

    def add_values(j, p):
        acc[...] += jnp.dot(p, vaug[chunk(j), :], preferred_element_type=F32)

    def new_values(t_ref, mx):
        p = weights(t_ref[...], mx[...])
        acc[...] = jnp.dot(p, vaug[PAIR:, :], preferred_element_type=F32)

    def as_rows(level):
        padded = jnp.concatenate([level, jnp.zeros((HD - BLOCK, HD), F32)], axis=0)
        row = jnp.transpose(padded)[0:8, :]
        high = row.astype(BF16).astype(F32)
        middle = (row - high).astype(BF16).astype(F32)
        low = row - high - middle
        place = lax.broadcasted_iota(jnp.int32, (8, HD), 0)
        terms = jnp.where(
            place == 0, high, jnp.where(place == 1, middle, jnp.where(place == 2, low, 0.0))
        )
        return jnp.concatenate([terms, jnp.zeros((8, HD), F32)], axis=0).astype(BF16)

    def result_copy(k, d, rel):
        return remote(nsend.at[k], nrecv.at[k], n_send.at[k], n_recv.at[k], device(d, rel, c))

    def finish(i, code, mx, maybe_first):
        total = acc[:, HD:]
        n = (acc[:, :HD] / total).astype(BF16)
        level = mx[...] * SCALE2 + jnp.log(total) * math.log2(math.e)
        for part in range(PARTS):
            rows = slice(part * BLOCK, (part + 1) * BLOCK)
            k = PARTS * i + part
            nsend[k, 0:BLOCK, :] = n[rows]
            nsend[k, BLOCK:, :] = as_rows(level[rows])
            copy = result_copy(k, (code // PLANES ** (part // 2)) % PLANES, part % 2)
            if maybe_first and part == 0:
                @pl.when(i > 0)
                def _():
                    copy.start()

                @pl.when(i == 0)
                def _():
                    nrecv[0] = nsend[0]
            else:
                copy.start()
        return code // PLANES**GROUP

    copy_k.wait()
    mask_keys(0)
    for copy in pair[:3]:
        copy.wait_recv()
    for part in range(1, PARTS):
        query_copy(part, 0, 1).wait_recv()
    q = queries_of(0)
    new_scores(True, q, t0, mx0)

    def first_scores(j, _):
        @pl.when(j == CHUNKS // 2)
        def _():
            pair[3].wait_recv()
            mask_keys(CACHE)

        scores(q, j, s0, mx0)
        return 0

    lax.fori_loop(0, CHUNKS, first_scores, 0)
    close_max(mx0)
    copy_v.wait()
    mask_values(0)

    def both(i, s_now, t_now, mx_now, s_later, t_later, mx_later, maybe_first):
        wait_queries(i + 1)
        q = queries_of(i + 1)
        new_scores(False, q, t_later, mx_later)
        new_values(t_now, mx_now)

        def body(j, _):
            if maybe_first:
                @pl.when((i == 0) & (j == CHUNKS // 2))
                def _():
                    pair[4].wait_recv()
                    mask_values(CACHE)

            p = chunk_weights(j, s_now, mx_now)
            scores(q, j, s_later, mx_later)
            add_values(j, p)
            return 0

        lax.fori_loop(0, CHUNKS, body, 0)
        close_max(mx_later)

    def two_tiles(k, code):
        i = 2 * k
        both(i, s0, t0, mx0, s1, t1, mx1, True)
        code = finish(i, code, mx0, True)

        @pl.when(i + 2 < TILES)
        def _():
            both(i + 1, s1, t1, mx1, s0, t0, mx0, False)

        @pl.when(i + 2 == TILES)
        def _():
            new_values(t1, mx1)

            def body(j, _):
                add_values(j, chunk_weights(j, s1, mx1))
                return 0

            lax.fori_loop(0, CHUNKS, body, 0)

        return finish(i + 1, code, mx1, False)

    lax.fori_loop(0, TILES // 2, two_tiles, CODE)

    def wait_result(k, _):
        result_copy(k, 0, 1).wait_recv()
        return 0

    def level_of(v):
        terms = nrecv[v, BLOCK:, :].astype(F32)
        return jnp.broadcast_to(jnp.sum(terms, axis=0, keepdims=True), (8, HD))

    def as_columns(rows):
        place = lax.broadcasted_iota(jnp.int32, (8, HD), 0)
        packed = []
        for first in range(0, len(rows), 8):
            block = jnp.zeros((8, HD), F32)
            for v in range(first, min(first + 8, len(rows))):
                block = jnp.where(place == v - first, rows[v], block)
            packed.append(block)
        packed.append(jnp.zeros((HD - 8 * len(packed), HD), F32))
        return jnp.transpose(jnp.concatenate(packed, axis=0))[0:BLOCK, :]

    def largest(levels):
        top = levels[0]
        for level in levels[1:]:
            top = jnp.maximum(top, level)
        return top

    early = SLOTS - PARTS
    lax.fori_loop(1, early, wait_result, 0)
    levels = [level_of(v) for v in range(early)]
    early_top = largest(levels)
    shares = [jnp.exp2(level - early_top) for level in levels]
    early_sum = sum(shares[1:], shares[0])
    share = as_columns(shares)
    early_total = jnp.zeros((BLOCK, HD), F32)
    for v in range(early):
        early_total = early_total + nrecv[v, 0:BLOCK, :].astype(F32) * share[:, v : v + 1]

    lax.fori_loop(early, SLOTS, wait_result, 0)
    levels = [early_top] + [level_of(v) for v in range(early, SLOTS)]
    summit = largest(levels)
    shares = [jnp.exp2(level - summit) for level in levels]
    denom = sum(shares[1:], shares[0] * early_sum)
    share = as_columns([part / denom for part in shares])
    attention = early_total * share[:, 0:1]
    for k in range(PARTS):
        part = nrecv[early + k, 0:BLOCK, :].astype(F32)
        attention = attention + part * share[:, k + 1 : k + 2]
    attention = attention.astype(BF16)
    for g in range(HEADS):
        flat[:, g * HD : (g + 1) * HD] = attention[g * ROWS : (g + 1) * ROWS, :]

    def wait_weights(k, _):
        weight_copy(k).wait()
        return 0

    lax.fori_loop(0, TP, wait_weights, 0)

    def columns(i):
        return remote(
            psend.at[i], precv.at[i], p_send.at[i], p_recv.at[i],
            {"work": me, "tp": (t + i) % TP},
        )

    joined = flat[...]
    for i in (4, 5, 3, 2, 6, 7, 1):
        psend[i] = jnp.dot(joined, wv[(t + i) % TP], preferred_element_type=F32).astype(BF16)
        columns(i).start()
    total = jnp.dot(joined, wv[t], preferred_element_type=F32)

    def gather(i, total):
        columns(i).wait_recv()
        return total + precv[i].astype(F32)

    out_ref[...] = lax.fori_loop(1, TP, gather, total).astype(BF16)

    for copy in pair:
        copy.wait_send()

    def sent(k, _):
        query_copy(k, 0, 1).wait_send()
        result_copy(k, 0, 1).wait_send()
        return 0

    lax.fori_loop(1, SLOTS, sent, 0)

    def sent_columns(i, _):
        columns(i).wait_send()
        return 0

    lax.fori_loop(1, TP, sent_columns, 0)


def per_device(
    queries, new_keys, new_values, cache_keys, cache_values, lengths, positions, out_weight
):
    vmem = pl.BlockSpec(memory_space=pltpu.VMEM)
    smem = pl.BlockSpec(memory_space=pltpu.SMEM)
    anywhere = pl.BlockSpec(memory_space=pl.ANY)
    dma = pltpu.SemaphoreType.DMA
    out = pl.pallas_call(
        kernel,
        out_shape=jax.ShapeDtypeStruct((ROWS, COLS), BF16),
        in_specs=[smem, smem, vmem, vmem, vmem, anywhere, anywhere, anywhere],
        out_specs=vmem,
        scratch_shapes=[
            pltpu.VMEM((PAIR + NEWPAD, HD), BF16),
            pltpu.VMEM((PAIR + NEWPAD, 2 * HD), BF16),
            pltpu.VMEM((TP, COLS, COLS), BF16),
            pltpu.VMEM((SLOTS, BLOCK, HD), BF16),
            pltpu.VMEM((SLOTS, MESSAGE, HD), BF16),
            pltpu.VMEM((SLOTS, MESSAGE, HD), BF16),
            pltpu.VMEM((CHUNKS, TILE, CHUNK), F32),
            pltpu.VMEM((CHUNKS, TILE, CHUNK), F32),
            pltpu.VMEM((TILE, HD), F32),
            pltpu.VMEM((TILE, HD), F32),
            pltpu.VMEM((TILE, HD), F32),
            pltpu.VMEM((TILE, HD), F32),
            pltpu.VMEM((TILE, 2 * HD), F32),
            pltpu.VMEM((ROWS, HEADS * HD), BF16),
            pltpu.VMEM((TP, ROWS, COLS), BF16),
            pltpu.VMEM((TP, ROWS, COLS), BF16),
            pltpu.VMEM((2, 8, HD), F32),
            dma((2 + TP,)),
            dma((5,)),
            dma((5,)),
            dma((SLOTS,)),
            dma((SLOTS,)),
            dma((SLOTS,)),
            dma((SLOTS,)),
            dma((TP,)),
            dma((TP,)),
        ],
        compiler_params=pltpu.CompilerParams(
            collective_id=0, has_side_effects=True, vmem_limit_bytes=58 * 1024 * 1024
        ),
    )(
        positions.reshape(ROWS),
        lengths,
        queries[0].transpose(1, 0, 2).reshape(BLOCK, HD),
        new_keys.reshape(ROWS, HD),
        new_values.reshape(ROWS, HD),
        cache_keys.reshape(CACHE, HD),
        cache_values.reshape(CACHE, HD),
        out_weight,
    )
    return out[None]


def solution(mesh):
    in_specs = (
        P("work", None, "tp", None),
        P("work", None, "tp", None),
        P("work", None, "tp", None),
        P("work", None, "tp", None),
        P("work", None, "tp", None),
        P("work"),
        P("work", None),
        P("tp", None),
    )
    out_specs = P("work", None, "tp")
    return jax.shard_map(
        per_device, mesh=mesh, in_specs=in_specs, out_specs=out_specs, check_vma=False
    )
```

profile of v0, /device:TPU:32, one launch (start us, length us, event | category | flops | bytes accessed | tf_op | source)
XLA Modules:
  0.0 49.1 jit_solution(15696831268873762127)
XLA Ops:
  0.7 47.1 %shard_map.82 = bf16[16,640]{1,0:T(8,128)(2,1)} custom-call(s32[16]{0:T(128)} %bitcast.17, s32[1]{0:T(128)S(6)} %copy.10.len_ref, bf16[80,128]{1,0:T(8,128)(2,1)} %bitcast.14, bf16[16,128]{1,0:T(8,128)(2,1)} %bitcast.15, bf16[16,128]{1,0:T(8,128)(2,1)} %bitcast.16, bf16[4096,128]{1,0:T(8,128)(2,1)} %bitcast.11, bf16[4096,128]{1,0:T(8,128)(2,1)} %bitcast.12, ...), custom_call_target="tpu_custom_call" | custom-call | tf_op jit(solution)/shard_map/pallas_call | solution.py:457
  47.8 1.3 %copy.11 = bf16[1,16,640]{2,1,0:T(8,128)(2,1)} copy(bf16[1,16,640]{2,1,0:T(8,128)(2,1)} %bitcast.13) | data formatting | bytes 40960
where the time goes:
time: 49.8 us; the launch traced here: 49.1 us
  Pallas kernels  47.1 us (95%)
  local copies, waits for them, and re-layouts  1.34 us (3%)
  between operations  0.66 us (1%)
    pallas_call x1, Pallas kernels, per_device(): pl.pallas_call(kernel, out_shape=jax.ShapeDtypeStruct((ROWS, COLS), BF16)...  47.1 us
    unnamed x1, local copies, waits for them, and re-layouts  1.34 us

commit v1 on v0

--- a/solution.py
+++ b/solution.py
@@ -28,8 +28,9 @@
 PLANES = 8
 TILES = PLANES // GROUP
 ORDER = (0, 7, 3, 5, 4, 2, 6, 1)
-CODE = sum(d * PLANES**i for i, d in enumerate(ORDER))
-SLOTS = 2 * PLANES
+BLOCKS = 1 + 2 * PLANES
+FIRST = ((2, 1 + PARTS), (0, 1 + PARTS))
+WIDEST = (1 + PARTS) * BLOCK
 MESSAGE = BLOCK + 16
 LEAST = 1024
 STEP = 1024
@@ -99,7 +100,7 @@
         signal(device(i // 2, i % 2, c))
         return 0
 
-    lax.fori_loop(1, SLOTS, greet, 0)
+    lax.fori_loop(1, BLOCKS - 1, greet, 0)
     signal(sibling)
 
     def greet_tp(i, _):
@@ -120,14 +121,17 @@
         return (x * cosine + pltpu.roll(x, HD // 2, 1) * sine).astype(BF16)
 
     for g in range(HEADS):
-        qbuf[0, g * ROWS : (g + 1) * ROWS, :] = rotated(q_ref[g * ROWS : (g + 1) * ROWS, :])
+        qbuf[1, g * ROWS : (g + 1) * ROWS, :] = rotated(q_ref[g * ROWS : (g + 1) * ROWS, :])
     kall[PAIR : PAIR + ROWS, :] = rotated(nk_ref[...])
     lens[0] = jnp.full((8, HD), len_ref[0], jnp.int32).astype(F32)
 
-    pl.semaphore_wait(barrier, SLOTS - 1 + 1 + TP - 1)
-
-    def query_copy(k, d, rel):
-        return remote(qbuf.at[0], qbuf.at[k], q_send.at[k], q_recv.at[k], device(-d, rel, c))
+    pl.semaphore_wait(barrier, 2 * PLANES - 1 + 1 + TP - 1)
+
+    def query_copy(k, to):
+        return remote(qbuf.at[1], qbuf.at[k], q_send.at[k], q_recv.at[k], to)
+
+    def on_core(core):
+        return pl.when(c == core)
 
     pair = [
         remote(src, dst, pair_send.at[k], pair_recv.at[k], sibling)
@@ -141,16 +145,17 @@
             )
         )
     ]
-    query_copy(1, 0, 1).start()
+    query_copy(2, partner).start()
+
+    @on_core(0)
+    def _():
+        query_copy(0, sibling).start()
+
     for copy in pair[:4]:
         copy.start()
-
-    def send_queries(i, code):
+    for i in range(1, PLANES):
         for rel in range(2):
-            query_copy(2 * i + rel, code % PLANES, rel).start()
-        return code // PLANES
-
-    lax.fori_loop(1, PLANES, send_queries, CODE // PLANES)
+            query_copy(1 + 2 * i + rel, device(-ORDER[i], rel, c)).start()
     pair[4].start()
 
     def weight_copy(k):
@@ -202,55 +207,68 @@
 
         lax.fori_loop(LEAST // STEP, CACHE // STEP, body, 0)
 
-    def wait_queries(i):
-        for part in range(PARTS):
-            query_copy(PARTS * i + part, 0, 1).wait_recv()
-
-    def queries_of(i):
-        return qbuf[pl.ds(PARTS * i, PARTS)].reshape(TILE, HD)
+    def tile_blocks(i):
+        return 1 + PARTS * i, 1 + PARTS * (i + 1)
+
+    def wait_queries(first, last):
+        for k in range(first, last):
+            if k != 1:
+                query_copy(k, partner).wait_recv()
+
+    def queries_of(first, last):
+        return qbuf[first:last].reshape((last - first) * BLOCK, HD)
 
     def chunk(j):
         return pl.ds(pl.multiple_of(j * CHUNK, CHUNK), CHUNK)
 
     def scores(q, j, s_ref, mx):
+        rows = q.shape[0]
         s = lax.dot_general(q, kall[chunk(j), :], NT, preferred_element_type=F32)
-        s_ref[j] = s
-        top = mx[...]
+        s_ref[j, 0:rows, :] = s
+        top = mx[0:rows, :]
         for u in range(CHUNK // HD):
             top = jnp.maximum(top, s[:, u * HD : (u + 1) * HD])
-        mx[...] = top
+        mx[0:rows, :] = top
 
     def new_scores(first, q, t_ref, mx):
-        row = lax.broadcasted_iota(jnp.int32, (TILE, HD), 0)
-        col = lax.broadcasted_iota(jnp.int32, (TILE, HD), 1)
+        rows = q.shape[0]
+        row = lax.broadcasted_iota(jnp.int32, (rows, HD), 0)
+        col = lax.broadcasted_iota(jnp.int32, (rows, HD), 1)
         r, r2 = row & 15, col & 15
         seen = (r2 >> 2) < (r >> 2)
-        if first:
-            own = (row < BLOCK) & (col < ROWS)
-            seen = seen | (own & ((r2 >> 2) == (r >> 2)) & (r2 <= r))
+        if first == 0:
+            sibling_own = (row < BLOCK) & (col >= ROWS)
+            mine = (row >= BLOCK) & (row < 2 * BLOCK) & (col < ROWS)
+            seen = seen | ((sibling_own | mine) & ((r2 >> 2) == (r >> 2)) & (r2 <= r))
         s = lax.dot_general(q, kall[PAIR:, :], NT, preferred_element_type=F32)
         s = jnp.where(seen & (col < 2 * ROWS), s, -1e30)
-        t_ref[...] = s
-        mx[...] = s
-
-    def close_max(mx):
-        mx[...] = jnp.broadcast_to(jnp.max(mx[...], axis=1, keepdims=True), (TILE, HD))
+        t_ref[0:rows, :] = s
+        mx[0:rows, :] = s
+
+    def close_max(rows, mx):
+        mx[0:rows, :] = jnp.broadcast_to(
+            jnp.max(mx[0:rows, :], axis=1, keepdims=True), (rows, HD)
+        )
 
     def weights(s, top):
         return jnp.exp2((s - top) * SCALE2).astype(BF16)
 
-    def chunk_weights(j, s_ref, mx):
-        top = mx[...]
+    def chunk_weights(rows, j, s_ref, mx):
+        top = mx[0:rows, :]
         return jnp.concatenate(
-            [weights(s_ref[j, :, u * HD : (u + 1) * HD], top) for u in range(CHUNK // HD)], axis=1
-        )
-
-    def add_values(j, p):
-        acc[...] += jnp.dot(p, vaug[chunk(j), :], preferred_element_type=F32)
-
-    def new_values(t_ref, mx):
-        p = weights(t_ref[...], mx[...])
-        acc[...] = jnp.dot(p, vaug[PAIR:, :], preferred_element_type=F32)
+            [
+                weights(s_ref[j, 0:rows, u * HD : (u + 1) * HD], top)
+                for u in range(CHUNK // HD)
+            ],
+            axis=1,
+        )
+
+    def add_values(rows, j, p):
+        acc[0:rows, :] += jnp.dot(p, vaug[chunk(j), :], preferred_element_type=F32)
+
+    def new_values(rows, t_ref, mx):
+        p = weights(t_ref[0:rows, :], mx[0:rows, :])
+        acc[0:rows, :] = jnp.dot(p, vaug[PAIR:, :], preferred_element_type=F32)
 
     def as_rows(level):
         padded = jnp.concatenate([level, jnp.zeros((HD - BLOCK, HD), F32)], axis=0)
@@ -264,100 +282,90 @@
         )
         return jnp.concatenate([terms, jnp.zeros((8, HD), F32)], axis=0).astype(BF16)
 
-    def result_copy(k, d, rel):
-        return remote(nsend.at[k], nrecv.at[k], n_send.at[k], n_recv.at[k], device(d, rel, c))
-
-    def finish(i, code, mx, maybe_first):
-        total = acc[:, HD:]
-        n = (acc[:, :HD] / total).astype(BF16)
-        level = mx[...] * SCALE2 + jnp.log(total) * math.log2(math.e)
-        for part in range(PARTS):
-            rows = slice(part * BLOCK, (part + 1) * BLOCK)
-            k = PARTS * i + part
-            nsend[k, 0:BLOCK, :] = n[rows]
-            nsend[k, BLOCK:, :] = as_rows(level[rows])
-            copy = result_copy(k, (code // PLANES ** (part // 2)) % PLANES, part % 2)
-            if maybe_first and part == 0:
-                @pl.when(i > 0)
-                def _():
-                    copy.start()
-
-                @pl.when(i == 0)
-                def _():
-                    nrecv[0] = nsend[0]
+    def result_copy(k, to, place=None):
+        place = k if place is None else place
+        return remote(nsend.at[k], nrecv.at[place], n_send.at[k], n_recv.at[place], to)
+
+    def finish(first, last, mx):
+        rows = (last - first) * BLOCK
+        total = acc[0:rows, HD:]
+        n = (acc[0:rows, :HD] / total).astype(BF16)
+        level = mx[0:rows, :] * SCALE2 + jnp.log(total) * math.log2(math.e)
+        for k in range(first, last):
+            part = slice((k - first) * BLOCK, (k - first + 1) * BLOCK)
+            nsend[k, 0:BLOCK, :] = n[part]
+            nsend[k, BLOCK:, :] = as_rows(level[part])
+            if k == 0:
+                result_copy(0, sibling, 1).start()
+            elif k == 1:
+                nrecv[1] = nsend[1]
             else:
-                copy.start()
-        return code // PLANES**GROUP
+                result_copy(k, device(ORDER[(k - 1) // 2], (k - 1) % 2, c)).start()
 
     copy_k.wait()
     mask_keys(0)
     for copy in pair[:3]:
         copy.wait_recv()
-    for part in range(1, PARTS):
-        query_copy(part, 0, 1).wait_recv()
-    q = queries_of(0)
-    new_scores(True, q, t0, mx0)
-
-    def first_scores(j, _):
-        @pl.when(j == CHUNKS // 2)
-        def _():
-            pair[3].wait_recv()
-            mask_keys(CACHE)
-
-        scores(q, j, s0, mx0)
-        return 0
-
-    lax.fori_loop(0, CHUNKS, first_scores, 0)
-    close_max(mx0)
+    for core in range(2):
+        @on_core(core)
+        def _(first=FIRST[core][0], last=FIRST[core][1]):
+            wait_queries(first, last)
+            q = queries_of(first, last)
+            new_scores(first, q, t0, mx0)
+
+            def body(j, _):
+                @pl.when(j == CHUNKS // 2)
+                def _():
+                    pair[3].wait_recv()
+                    mask_keys(CACHE)
+
+                scores(q, j, s0, mx0)
+                return 0
+
+            lax.fori_loop(0, CHUNKS, body, 0)
+            close_max(q.shape[0], mx0)
+
     copy_v.wait()
     mask_values(0)
 
-    def both(i, s_now, t_now, mx_now, s_later, t_later, mx_later, maybe_first):
-        wait_queries(i + 1)
-        q = queries_of(i + 1)
-        new_scores(False, q, t_later, mx_later)
-        new_values(t_now, mx_now)
+    def step(i, first, last):
+        s_now, t_now, mx_now = ((s0, t0, mx0), (s1, t1, mx1))[i % 2]
+        s_later, t_later, mx_later = ((s1, t1, mx1), (s0, t0, mx0))[i % 2]
+        rows = (last - first) * BLOCK
+        if i + 1 < TILES:
+            wait_queries(*tile_blocks(i + 1))
+            q = queries_of(*tile_blocks(i + 1))
+            new_scores(tile_blocks(i + 1)[0], q, t_later, mx_later)
+        new_values(rows, t_now, mx_now)
 
         def body(j, _):
-            if maybe_first:
-                @pl.when((i == 0) & (j == CHUNKS // 2))
+            if i == 0:
+                @pl.when(j == CHUNKS // 2)
                 def _():
                     pair[4].wait_recv()
                     mask_values(CACHE)
 
-            p = chunk_weights(j, s_now, mx_now)
-            scores(q, j, s_later, mx_later)
-            add_values(j, p)
+            p = chunk_weights(rows, j, s_now, mx_now)
+            if i + 1 < TILES:
+                scores(q, j, s_later, mx_later)
+            add_values(rows, j, p)
             return 0
 
         lax.fori_loop(0, CHUNKS, body, 0)
-        close_max(mx_later)
-
-    def two_tiles(k, code):
-        i = 2 * k
-        both(i, s0, t0, mx0, s1, t1, mx1, True)
-        code = finish(i, code, mx0, True)
-
-        @pl.when(i + 2 < TILES)
-        def _():
-            both(i + 1, s1, t1, mx1, s0, t0, mx0, False)
-
-        @pl.when(i + 2 == TILES)
-        def _():
-            new_values(t1, mx1)
-
-            def body(j, _):
-                add_values(j, chunk_weights(j, s1, mx1))
-                return 0
-
-            lax.fori_loop(0, CHUNKS, body, 0)
-
-        return finish(i + 1, code, mx1, False)
-
-    lax.fori_loop(0, TILES // 2, two_tiles, CODE)
+        if i + 1 < TILES:
+            close_max(q.shape[0], mx_later)
+        finish(first, last, mx_now)
+
+    for core in range(2):
+        @on_core(core)
+        def _(first=FIRST[core][0], last=FIRST[core][1]):
+            step(0, first, last)
+
+    for i in range(1, TILES):
+        step(i, *tile_blocks(i))
 
     def wait_result(k, _):
-        result_copy(k, 0, 1).wait_recv()
+        result_copy(k, partner).wait_recv()
         return 0
 
     def level_of(v):
@@ -381,19 +389,24 @@
             top = jnp.maximum(top, level)
         return top
 
-    early = SLOTS - PARTS
-    lax.fori_loop(1, early, wait_result, 0)
-    levels = [level_of(v) for v in range(early)]
+    early = BLOCKS - PARTS
+
+    @on_core(0)
+    def _():
+        wait_result(1, 0)
+
+    lax.fori_loop(2, early, wait_result, 0)
+    levels = [level_of(v) for v in range(1, early)]
     early_top = largest(levels)
     shares = [jnp.exp2(level - early_top) for level in levels]
     early_sum = sum(shares[1:], shares[0])
     share = as_columns(shares)
     early_total = jnp.zeros((BLOCK, HD), F32)
-    for v in range(early):
-        early_total = early_total + nrecv[v, 0:BLOCK, :].astype(F32) * share[:, v : v + 1]
-
-    lax.fori_loop(early, SLOTS, wait_result, 0)
-    levels = [early_top] + [level_of(v) for v in range(early, SLOTS)]
+    for v in range(1, early):
+        early_total = early_total + nrecv[v, 0:BLOCK, :].astype(F32) * share[:, v - 1 : v]
+
+    lax.fori_loop(early, BLOCKS, wait_result, 0)
+    levels = [early_top] + [level_of(v) for v in range(early, BLOCKS)]
     summit = largest(levels)
     shares = [jnp.exp2(level - summit) for level in levels]
     denom = sum(shares[1:], shares[0] * early_sum)
@@ -434,11 +447,20 @@
         copy.wait_send()
 
     def sent(k, _):
-        query_copy(k, 0, 1).wait_send()
-        result_copy(k, 0, 1).wait_send()
-        return 0
-
-    lax.fori_loop(1, SLOTS, sent, 0)
+        query_copy(k, partner).wait_send()
+        result_copy(k, partner).wait_send()
+        return 0
+
+    lax.fori_loop(2, BLOCKS, sent, 0)
+
+    @on_core(0)
+    def _():
+        query_copy(0, sibling).wait_send()
+
+    @on_core(1)
+    def _():
+        result_copy(0, sibling, 1).wait_send()
+
 
     def sent_columns(i, _):
         columns(i).wait_send()
@@ -463,16 +485,16 @@
             pltpu.VMEM((PAIR + NEWPAD, HD), BF16),
             pltpu.VMEM((PAIR + NEWPAD, 2 * HD), BF16),
             pltpu.VMEM((TP, COLS, COLS), BF16),
-            pltpu.VMEM((SLOTS, BLOCK, HD), BF16),
-            pltpu.VMEM((SLOTS, MESSAGE, HD), BF16),
-            pltpu.VMEM((SLOTS, MESSAGE, HD), BF16),
+            pltpu.VMEM((BLOCKS, BLOCK, HD), BF16),
+            pltpu.VMEM((BLOCKS, MESSAGE, HD), BF16),
+            pltpu.VMEM((BLOCKS, MESSAGE, HD), BF16),
+            pltpu.VMEM((CHUNKS, WIDEST, CHUNK), F32),
             pltpu.VMEM((CHUNKS, TILE, CHUNK), F32),
-            pltpu.VMEM((CHUNKS, TILE, CHUNK), F32),
+            pltpu.VMEM((WIDEST, HD), F32),
             pltpu.VMEM((TILE, HD), F32),
+            pltpu.VMEM((WIDEST, HD), F32),
             pltpu.VMEM((TILE, HD), F32),
-            pltpu.VMEM((TILE, HD), F32),
-            pltpu.VMEM((TILE, HD), F32),
-            pltpu.VMEM((TILE, 2 * HD), F32),
+            pltpu.VMEM((WIDEST, 2 * HD), F32),
             pltpu.VMEM((ROWS, HEADS * HD), BF16),
             pltpu.VMEM((TP, ROWS, COLS), BF16),
             pltpu.VMEM((TP, ROWS, COLS), BF16),
@@ -480,10 +502,10 @@
             dma((2 + TP,)),
             dma((5,)),
             dma((5,)),
-            dma((SLOTS,)),
-            dma((SLOTS,)),
-            dma((SLOTS,)),
-            dma((SLOTS,)),
+            dma((BLOCKS,)),
+            dma((BLOCKS,)),
+            dma((BLOCKS,)),
+            dma((BLOCKS,)),
             dma((TP,)),
             dma((TP,)),
         ],

time: 49.8 us -> 49.9 us (level)
  Pallas kernels: 47.1 us -> 47.6 us
    pallas_call x1, Pallas kernels: 47.1 us -> 47.6 us  [per_device(): pl.pallas_call(kernel, out_shape=jax.ShapeDtypeStruct((ROWS, COLS), BF16)...]
where the time goes in v1:
time: 49.9 us; the launch traced here: 49.6 us
  Pallas kernels  47.6 us (95%)
  local copies, waits for them, and re-layouts  1.34 us (3%)
  between operations  0.66 us (1%)
    pallas_call x1, Pallas kernels, per_device(): pl.pallas_call(kernel, out_shape=jax.ShapeDtypeStruct((ROWS, COLS), BF16)...  47.6 us
    unnamed x1, local copies, waits for them, and re-layouts  1.34 us

profile of v1, /device:TPU:32, one launch (start us, length us, event | category | flops | bytes accessed | tf_op | source)
XLA Modules:
  0.0 49.6 jit_solution(8595229852501311075)
XLA Ops:
  0.7 47.6 %shard_map.82 = bf16[16,640]{1,0:T(8,128)(2,1)} custom-call(s32[16]{0:T(128)} %bitcast.17, s32[1]{0:T(128)S(6)} %copy.10.len_ref, bf16[80,128]{1,0:T(8,128)(2,1)} %bitcast.14, bf16[16,128]{1,0:T(8,128)(2,1)} %bitcast.15, bf16[16,128]{1,0:T(8,128)(2,1)} %bitcast.16, bf16[4096,128]{1,0:T(8,128)(2,1)} %bitcast.11, bf16[4096,128]{1,0:T(8,128)(2,1)} %bitcast.12, ...), custom_call_target="tpu_custom_call" | custom-call | tf_op jit(solution)/shard_map/pallas_call | solution.py:479
  48.3 1.3 %copy.11 = bf16[1,16,640]{2,1,0:T(8,128)(2,1)} copy(bf16[1,16,640]{2,1,0:T(8,128)(2,1)} %bitcast.13) | data formatting | bytes 40960

commit v2 on v0

--- a/solution.py
+++ b/solution.py
@@ -27,7 +27,7 @@
 COLS = 640
 PLANES = 8
 TILES = PLANES // GROUP
-ORDER = (0, 7, 3, 5, 4, 2, 6, 1)
+ORDER = (0, 2, 4, 6, 3, 5, 1, 7)
 CODE = sum(d * PLANES**i for i, d in enumerate(ORDER))
 SLOTS = 2 * PLANES
 MESSAGE = BLOCK + 16
@@ -141,17 +141,16 @@
             )
         )
     ]
+    def send_queries(first, last):
+        for i in range(first, last):
+            for rel in range(2):
+                query_copy(2 * i + rel, ORDER[i], rel).start()
+
     query_copy(1, 0, 1).start()
-    for copy in pair[:4]:
+    send_queries(1, 2 * GROUP)
+    for copy in pair:
         copy.start()
-
-    def send_queries(i, code):
-        for rel in range(2):
-            query_copy(2 * i + rel, code % PLANES, rel).start()
-        return code // PLANES
-
-    lax.fori_loop(1, PLANES, send_queries, CODE // PLANES)
-    pair[4].start()
+    send_queries(2 * GROUP, PLANES)
 
     def weight_copy(k):
         return pltpu.make_async_copy(

time: 49.8 us -> 50.9 us (1.022)
  Pallas kernels: 47.1 us -> 48.7 us
    pallas_call x1, Pallas kernels: 47.1 us -> 48.7 us  [per_device(): pl.pallas_call(kernel, out_shape=jax.ShapeDtypeStruct((ROWS, COLS), BF16)...]
where the time goes in v2:
time: 50.9 us; the launch traced here: 50.7 us
  Pallas kernels  48.7 us (96%)
  local copies, waits for them, and re-layouts  1.34 us (3%)
  between operations  0.66 us (1%)
    pallas_call x1, Pallas kernels, per_device(): pl.pallas_call(kernel, out_shape=jax.ShapeDtypeStruct((ROWS, COLS), BF16)...  48.7 us
    unnamed x1, local copies, waits for them, and re-layouts  1.34 us

profile of v2, /device:TPU:32, one launch (start us, length us, event | category | flops | bytes accessed | tf_op | source)
XLA Modules:
  0.0 50.7 jit_solution(9638192826805178813)
XLA Ops:
  0.7 48.7 %shard_map.82 = bf16[16,640]{1,0:T(8,128)(2,1)} custom-call(s32[16]{0:T(128)} %bitcast.17, s32[1]{0:T(128)S(6)} %copy.10.len_ref, bf16[80,128]{1,0:T(8,128)(2,1)} %bitcast.14, bf16[16,128]{1,0:T(8,128)(2,1)} %bitcast.15, bf16[16,128]{1,0:T(8,128)(2,1)} %bitcast.16, bf16[4096,128]{1,0:T(8,128)(2,1)} %bitcast.11, bf16[4096,128]{1,0:T(8,128)(2,1)} %bitcast.12, ...), custom_call_target="tpu_custom_call" | custom-call | tf_op jit(solution)/shard_map/pallas_call | solution.py:456
  49.3 1.3 %copy.11 = bf16[1,16,640]{2,1,0:T(8,128)(2,1)} copy(bf16[1,16,640]{2,1,0:T(8,128)(2,1)} %bitcast.13) | data formatting | bytes 40960

commit v3 on v0

--- a/solution.py
+++ b/solution.py
@@ -124,6 +124,37 @@
     kall[PAIR : PAIR + ROWS, :] = rotated(nk_ref[...])
     lens[0] = jnp.full((8, HD), len_ref[0], jnp.int32).astype(F32)
 
+    def live_rows(owner, j):
+        rows = lax.broadcasted_iota(jnp.int32, (STEP, HD), 0) + j * STEP
+        return jnp.where(rows.astype(F32) < lens[owner, 0:1, :], 1.0, 0.0).astype(BF16)
+
+    def mark_live(owner):
+        def body(j, _):
+            rows = pl.ds(owner * CACHE + pl.multiple_of(j * STEP, STEP), STEP)
+            vaug[rows, HD:] = live_rows(owner, j)
+            return 0
+
+        lax.fori_loop(0, CACHE // STEP, body, 0)
+
+    def mask_keys(j, _):
+        live = live_rows(0, j)
+        rows = pl.ds(pl.multiple_of(j * STEP, STEP), STEP)
+        kall[rows, :] = kall[rows, :] * live + head_key * (1.0 - live)
+        return 0
+
+    def mask_values(j, _):
+        rows = pl.ds(pl.multiple_of(j * STEP, STEP), STEP)
+        vaug[rows, 0:HD] = vaug[rows, 0:HD] * live_rows(0, j)
+        return 0
+
+    copy_k.wait()
+    head_key = kall[0:16, :].astype(F32)[0:1, :]
+    head_key = jnp.broadcast_to(head_key, (STEP, HD)).astype(BF16)
+    lax.fori_loop(LEAST // STEP, CACHE // STEP, mask_keys, 0)
+    copy_v.wait()
+    lax.fori_loop(LEAST // STEP, CACHE // STEP, mask_values, 0)
+    mark_live(0)
+
     pl.semaphore_wait(barrier, SLOTS - 1 + 1 + TP - 1)
 
     def query_copy(k, d, rel):
@@ -136,8 +167,11 @@
                 (lens.at[0], lens.at[1]),
                 (kall.at[pl.ds(PAIR, ROWS)], kall.at[pl.ds(PAIR + ROWS, ROWS)]),
                 (nv_ref, vaug.at[pl.ds(PAIR + ROWS, ROWS), pl.ds(0, HD)]),
-                (ck_ref, kall.at[pl.ds(CACHE, CACHE)]),
-                (cv_ref, vaug.at[pl.ds(CACHE, CACHE), pl.ds(0, HD)]),
+                (kall.at[pl.ds(0, CACHE)], kall.at[pl.ds(CACHE, CACHE)]),
+                (
+                    vaug.at[pl.ds(0, CACHE), pl.ds(0, HD)],
+                    vaug.at[pl.ds(CACHE, CACHE), pl.ds(0, HD)],
+                ),
             )
         )
     ]
@@ -168,39 +202,6 @@
     vaug[PAIR : PAIR + ROWS, 0:HD] = nv_ref[...]
     vaug[PAIR + 2 * ROWS :, 0:HD] = jnp.zeros((NEWPAD - 2 * ROWS, HD), BF16)
     vaug[PAIR:, HD:] = jnp.ones((NEWPAD, HD), BF16)
-
-    def live_rows(base, j):
-        rows = lax.broadcasted_iota(jnp.int32, (STEP, HD), 0) + j * STEP
-        return jnp.where(rows.astype(F32) < lens[base // CACHE, 0:1, :], 1.0, 0.0).astype(BF16)
-
-    def mask_keys(base):
-        first = kall[base : base + 16, :].astype(F32)[0:1, :]
-        first = jnp.broadcast_to(first, (STEP, HD)).astype(BF16)
-
-        def body(j, _):
-            live = live_rows(base, j)
-            rows = pl.ds(base + pl.multiple_of(j * STEP, STEP), STEP)
-            kall[rows, :] = kall[rows, :] * live + first * (1.0 - live)
-            return 0
-
-        lax.fori_loop(LEAST // STEP, CACHE // STEP, body, 0)
-
-    def mask_values(base):
-        def ones(j, _):
-            rows = pl.ds(base + pl.multiple_of(j * STEP, STEP), STEP)
-            vaug[rows, HD:] = jnp.ones((STEP, HD), BF16)
-            return 0
-
-        lax.fori_loop(0, LEAST // STEP, ones, 0)
-
-        def body(j, _):
-            live = live_rows(base, j)
-            rows = pl.ds(base + pl.multiple_of(j * STEP, STEP), STEP)
-            vaug[rows, 0:HD] = vaug[rows, 0:HD] * live
-            vaug[rows, HD:] = live
-            return 0
-
-        lax.fori_loop(LEAST // STEP, CACHE // STEP, body, 0)
 
     def wait_queries(i):
         for part in range(PARTS):
@@ -289,8 +290,6 @@
                 copy.start()
         return code // PLANES**GROUP
 
-    copy_k.wait()
-    mask_keys(0)
     for copy in pair[:3]:
         copy.wait_recv()
     for part in range(1, PARTS):
@@ -301,17 +300,14 @@
     def first_scores(j, _):
         @pl.when(j == CHUNKS // 2)
         def _():
+            mark_live(1)
             pair[3].wait_recv()
-            mask_keys(CACHE)
 
         scores(q, j, s0, mx0)
         return 0
 
     lax.fori_loop(0, CHUNKS, first_scores, 0)
     close_max(mx0)
-    copy_v.wait()
-    mask_values(0)
-
     def both(i, s_now, t_now, mx_now, s_later, t_later, mx_later, maybe_first):
         wait_queries(i + 1)
         q = queries_of(i + 1)
@@ -323,7 +319,6 @@
                 @pl.when((i == 0) & (j == CHUNKS // 2))
                 def _():
                     pair[4].wait_recv()
-                    mask_values(CACHE)
 
             p = chunk_weights(j, s_now, mx_now)
             scores(q, j, s_later, mx_later)

time: 49.8 us -> 48.8 us (0.980); the launches traced: 49.1 us -> 48.6 us
  Pallas kernels: 47.1 us -> 46.6 us
where the time goes in v3:
time: 48.8 us; the launch traced here: 48.6 us
  Pallas kernels  46.6 us (95%)
  local copies, waits for them, and re-layouts  1.34 us (3%)
  between operations  0.66 us (1%)
    pallas_call x1, Pallas kernels, per_device(): pl.pallas_call(kernel, out_shape=jax.ShapeDtypeStruct((ROWS, COLS), BF16)...  46.6 us
    unnamed x1, local copies, waits for them, and re-layouts  1.34 us

profile of v3, /device:TPU:32, one launch (start us, length us, event | category | flops | bytes accessed | tf_op | source)
XLA Modules:
  0.0 48.6 jit_solution(16679825597001651749)
XLA Ops:
  0.7 46.6 %shard_map.82 = bf16[16,640]{1,0:T(8,128)(2,1)} custom-call(s32[16]{0:T(128)} %bitcast.17, s32[1]{0:T(128)S(6)} %copy.10.len_ref, bf16[80,128]{1,0:T(8,128)(2,1)} %bitcast.14, bf16[16,128]{1,0:T(8,128)(2,1)} %bitcast.15, bf16[16,128]{1,0:T(8,128)(2,1)} %bitcast.16, bf16[4096,128]{1,0:T(8,128)(2,1)} %bitcast.11, bf16[4096,128]{1,0:T(8,128)(2,1)} %bitcast.12, ...), custom_call_target="tpu_custom_call" | custom-call | tf_op jit(solution)/shard_map/pallas_call | solution.py:452
  47.3 1.3 %copy.11 = bf16[1,16,640]{2,1,0:T(8,128)(2,1)} copy(bf16[1,16,640]{2,1,0:T(8,128)(2,1)} %bitcast.13) | data formatting | bytes 40960

commit v4 on v3

--- a/solution.py
+++ b/solution.py
@@ -167,16 +167,23 @@
                 (lens.at[0], lens.at[1]),
                 (kall.at[pl.ds(PAIR, ROWS)], kall.at[pl.ds(PAIR + ROWS, ROWS)]),
                 (nv_ref, vaug.at[pl.ds(PAIR + ROWS, ROWS), pl.ds(0, HD)]),
-                (kall.at[pl.ds(0, CACHE)], kall.at[pl.ds(CACHE, CACHE)]),
-                (
-                    vaug.at[pl.ds(0, CACHE), pl.ds(0, HD)],
-                    vaug.at[pl.ds(CACHE, CACHE), pl.ds(0, HD)],
-                ),
+                *[
+                    (kall.at[pl.ds(r, CHUNK)], kall.at[pl.ds(CACHE + r, CHUNK)])
+                    for r in range(0, CACHE, CHUNK)
+                ],
+                *[
+                    (
+                        vaug.at[pl.ds(r, CHUNK), pl.ds(0, HD)],
+                        vaug.at[pl.ds(CACHE + r, CHUNK), pl.ds(0, HD)],
+                    )
+                    for r in range(0, CACHE, CHUNK)
+                ],
             )
         )
     ]
     query_copy(1, 0, 1).start()
-    for copy in pair[:4]:
+    pair_keys, pair_values = pair[3 : 3 + CHUNKS // 2], pair[3 + CHUNKS // 2 :]
+    for copy in pair[:3] + pair_keys:
         copy.start()
 
     def send_queries(i, code):
@@ -185,7 +192,8 @@
         return code // PLANES
 
     lax.fori_loop(1, PLANES, send_queries, CODE // PLANES)
-    pair[4].start()
+    for copy in pair_values:
+        copy.start()
 
     def weight_copy(k):
         return pltpu.make_async_copy(
@@ -301,7 +309,9 @@
         @pl.when(j == CHUNKS // 2)
         def _():
             mark_live(1)
-            pair[3].wait_recv()
+
+        for k, copy in enumerate(pair_keys):
+            pl.when(j == CHUNKS // 2 + k)(copy.wait_recv)
 
         scores(q, j, s0, mx0)
         return 0
@@ -316,9 +326,8 @@
 
         def body(j, _):
             if maybe_first:
-                @pl.when((i == 0) & (j == CHUNKS // 2))
-                def _():
-                    pair[4].wait_recv()
+                for k, copy in enumerate(pair_values):
+                    pl.when((i == 0) & (j == CHUNKS // 2 + k))(copy.wait_recv)
 
             p = chunk_weights(j, s_now, mx_now)
             scores(q, j, s_later, mx_later)
@@ -473,8 +482,8 @@
             pltpu.VMEM((TP, ROWS, COLS), BF16),
             pltpu.VMEM((2, 8, HD), F32),
             dma((2 + TP,)),
-            dma((5,)),
-            dma((5,)),
+            dma((3 + CHUNKS,)),
+            dma((3 + CHUNKS,)),
             dma((SLOTS,)),
             dma((SLOTS,)),
             dma((SLOTS,)),

time: 48.8 us -> 48.8 us (level)
  no operation moved by 1% of the time
where the time goes in v4:
time: 48.8 us; the launch traced here: 48.6 us
  Pallas kernels  46.6 us (95%)
  local copies, waits for them, and re-layouts  1.34 us (3%)
  between operations  0.66 us (1%)
    pallas_call x1, Pallas kernels, per_device(): pl.pallas_call(kernel, out_shape=jax.ShapeDtypeStruct((ROWS, COLS), BF16)...  46.6 us
    unnamed x1, local copies, waits for them, and re-layouts  1.34 us

profile of v4, /device:TPU:32, one launch (start us, length us, event | category | flops | bytes accessed | tf_op | source)
XLA Modules:
  0.0 48.6 jit_solution(13799557227574882331)
XLA Ops:
  0.7 46.6 %shard_map.82 = bf16[16,640]{1,0:T(8,128)(2,1)} custom-call(s32[16]{0:T(128)} %bitcast.17, s32[1]{0:T(128)S(6)} %copy.10.len_ref, bf16[80,128]{1,0:T(8,128)(2,1)} %bitcast.14, bf16[16,128]{1,0:T(8,128)(2,1)} %bitcast.15, bf16[16,128]{1,0:T(8,128)(2,1)} %bitcast.16, bf16[4096,128]{1,0:T(8,128)(2,1)} %bitcast.11, bf16[4096,128]{1,0:T(8,128)(2,1)} %bitcast.12, ...), custom_call_target="tpu_custom_call" | custom-call | tf_op jit(solution)/shard_map/pallas_call | solution.py:461
  47.3 1.3 %copy.11 = bf16[1,16,640]{2,1,0:T(8,128)(2,1)} copy(bf16[1,16,640]{2,1,0:T(8,128)(2,1)} %bitcast.13) | data formatting | bytes 40960

commit v5 on v4

--- a/solution.py
+++ b/solution.py
@@ -191,9 +191,10 @@
             query_copy(2 * i + rel, code % PLANES, rel).start()
         return code // PLANES
 
-    lax.fori_loop(1, PLANES, send_queries, CODE // PLANES)
+    code = lax.fori_loop(1, 2 * GROUP, send_queries, CODE // PLANES)
     for copy in pair_values:
         copy.start()
+    lax.fori_loop(2 * GROUP, PLANES, send_queries, code)
 
     def weight_copy(k):
         return pltpu.make_async_copy(

time: 48.8 us -> 48.8 us (level)
  no operation moved by 1% of the time
where the time goes in v5:
time: 48.8 us; the launch traced here: 48.6 us
  Pallas kernels  46.6 us (95%)
  local copies, waits for them, and re-layouts  1.34 us (3%)
  between operations  0.66 us (1%)
    pallas_call x1, Pallas kernels, per_device(): pl.pallas_call(kernel, out_shape=jax.ShapeDtypeStruct((ROWS, COLS), BF16)...  46.6 us
    unnamed x1, local copies, waits for them, and re-layouts  1.34 us

profile of v5, /device:TPU:32, one launch (start us, length us, event | category | flops | bytes accessed | tf_op | source)
XLA Modules:
  0.0 48.6 jit_solution(2828120327632803855)
XLA Ops:
  0.7 46.6 %shard_map.82 = bf16[16,640]{1,0:T(8,128)(2,1)} custom-call(s32[16]{0:T(128)} %bitcast.17, s32[1]{0:T(128)S(6)} %copy.10.len_ref, bf16[80,128]{1,0:T(8,128)(2,1)} %bitcast.14, bf16[16,128]{1,0:T(8,128)(2,1)} %bitcast.15, bf16[16,128]{1,0:T(8,128)(2,1)} %bitcast.16, bf16[4096,128]{1,0:T(8,128)(2,1)} %bitcast.11, bf16[4096,128]{1,0:T(8,128)(2,1)} %bitcast.12, ...), custom_call_target="tpu_custom_call" | custom-call | tf_op jit(solution)/shard_map/pallas_call | solution.py:462
  47.2 1.3 %copy.11 = bf16[1,16,640]{2,1,0:T(8,128)(2,1)} copy(bf16[1,16,640]{2,1,0:T(8,128)(2,1)} %bitcast.13) | data formatting | bytes 40960
